TPU v7x, 128 devices: a whole 4x4x4 slice. The times are simulated.
128 devices in a mesh: row: 8 (over x, y_hi), col: 4 (over y_lo, core), depth: 4 (over z).
Axes of the slice: x: 4, y: 4 (y_hi: 2, y_lo: 2; y = y_hi * 2 + y_lo), z: 4, core: 2. Of those that a mesh axis runs over, the one named last changes fastest.
Arguments:
- tokens: bfloat16 [768, 8192], P(('depth', 'col'), 'row'), may hold values from -6 to 6
- gate_weight: bfloat16 [8192, 14336], P('row', ('col', 'depth')), may hold values from -0.0625 to 0.0625
- up_weight: bfloat16 [8192, 14336], P('row', ('col', 'depth')), may hold values from -0.0625 to 0.0625
- down_weight: bfloat16 [14336, 8192], P(('col', 'depth'), 'row'), may hold values from -0.046875 to 0.046875
- cotangent: bfloat16 [768, 8192], P(('depth', 'col'), 'row'), may hold values from -0.86328125 to 0.86328125
Outputs:
- mixed: float32 [768, 8192], P(('depth', 'col'), 'row')
- token_grad: float32 [768, 8192], P(('depth', 'col'), 'row')
- gate_weight_grad: float32 [8192, 14336], P('row', ('col', 'depth'))
- up_weight_grad: float32 [8192, 14336], P('row', ('col', 'depth'))
- down_weight_grad: float32 [14336, 8192], P(('col', 'depth'), 'row')
All inputs are finite; a program needn't handle non-finite values.
Results may differ from a plain program's by a relative error of at most 0.012.
Values may be sent and summed in bfloat16 or wider, within the bound.
A program may use at most 192 MiB of HBM per device.

v0:
```python
import jax
import jax.numpy as jnp
from jax import lax
from jax.sharding import PartitionSpec as P


def swish_parts(gate):
    sigma_gate = jax.nn.sigmoid(gate)
    return (gate * sigma_gate, sigma_gate)


def product(left_side, right_side):
    return jnp.dot(left_side, right_side, preferred_element_type=jnp.float32)


def product_transposed(left_side, right_side):
    return lax.dot_general(
        left_side, right_side, (((1,), (1,)), ((), ())), preferred_element_type=jnp.float32
    )


def rounded_partial(left_side, right_side):
    partial_term = lax.dot_general(
        left_side, right_side, (((0,), (0,)), ((), ())), preferred_element_type=jnp.float32
    ).astype(jnp.bfloat16)
    return lax.optimization_barrier(partial_term).astype(jnp.float32)


def body(tokens, gate_weight, up_weight, down_weight, cotangent):
    gate_panel, up_panel, down_panel = (
        lax.all_gather(gate_weight, "depth", axis=1, tiled=True),
        lax.all_gather(up_weight, "depth", axis=1, tiled=True),
        lax.all_gather(down_weight, "depth", axis=0, tiled=True),
    )
    token_all, cotangent_all = (
        lax.all_gather(tokens, "col", axis=0, tiled=True),
        lax.all_gather(cotangent, "col", axis=0, tiled=True),
    )
    panel_width = gate_panel.shape[1]
    segment = token_all
    paired = lax.psum_scatter(
        jnp.concatenate([product(segment, gate_panel), product(segment, up_panel)], axis=1),
        "row",
        scatter_dimension=0,
        tiled=True,
    )
    gate_mine = paired[:, :panel_width]
    up_mine = paired[:, panel_width:]
    activated_mine, sigma_mine = swish_parts(gate_mine)
    hidden_mine = (activated_mine * up_mine).astype(jnp.bfloat16)
    hidden_all = lax.all_gather(hidden_mine, "row", axis=0, tiled=True)
    segment = hidden_all
    mixed = lax.psum_scatter(product(segment, down_panel), "col", scatter_dimension=0, tiled=True)
    segment = cotangent_all
    hidden_grad = lax.psum_scatter(
        product_transposed(segment, down_panel), "row", scatter_dimension=0, tiled=True
    )
    activated, sigma_gate = swish_parts(gate_mine)
    gate_grad = (
        hidden_grad * up_mine * sigma_gate * (1.0 + gate_mine * (1.0 - sigma_gate))
    ).astype(jnp.bfloat16)
    up_grad = (hidden_grad * activated).astype(jnp.bfloat16)
    gate_grad_all, up_grad_all = (
        lax.all_gather(gate_grad, "row", axis=0, tiled=True),
        lax.all_gather(up_grad, "row", axis=0, tiled=True),
    )
    token_grad = lax.psum_scatter(
        product_transposed(gate_grad_all, gate_panel) + product_transposed(up_grad_all, up_panel),
        "col",
        scatter_dimension=0,
        tiled=True,
    )
    gate_total, up_total, down_total = (
        lax.psum_scatter(
            rounded_partial(token_all, gate_grad_all).astype(jnp.bfloat16),
            "depth",
            scatter_dimension=1,
            tiled=True,
        ).astype(jnp.float32),
        lax.psum_scatter(
            rounded_partial(token_all, up_grad_all).astype(jnp.bfloat16),
            "depth",
            scatter_dimension=1,
            tiled=True,
        ).astype(jnp.float32),
        lax.psum_scatter(
            rounded_partial(hidden_all, cotangent_all).astype(jnp.bfloat16),
            "depth",
            scatter_dimension=0,
            tiled=True,
        ).astype(jnp.float32),
    )
    return (mixed, token_grad, gate_total, up_total, down_total)


def solution(mesh):
    placed = (
        P(("depth", "col"), "row"),
        P("row", ("col", "depth")),
        P("row", ("col", "depth")),
        P(("col", "depth"), "row"),
        P(("depth", "col"), "row"),
    )
    return jax.shard_map(
        body,
        mesh=mesh,
        in_specs=placed,
        out_specs=(
            P(("depth", "col"), "row"),
            P(("depth", "col"), "row"),
            P("row", ("col", "depth")),
            P("row", ("col", "depth")),
            P(("col", "depth"), "row"),
        ),
        check_vma=False,
    )
```

profile of v0, /device:TPU:1, one launch (start us, length us, event | category | flops | bytes accessed | tf_op | source)
XLA Modules:
  0.0 851.8 jit_solution(14917106579077975061)
XLA Ops:
  8.0 0.7 all-gather.7.cloned.1.call-update
  9.4 7.9 all_gather.29
  17.3 70.2 %all-gather.13.cloned.1.call-done = bf16[3584,1024]{1,0:T(8,128)(2,1)} async-done(((bf16[896,1024]{1,0:T(8,128)(2,1)}), bf16[3584,1024]{1,0:T(8,128)(2,1)}) %all-gather.13.cloned.1.call-update) | async-done | bytes 7340048 | tf_op jit(solution)/shard_map/all_gather | solution.py:33
  87.5 7.2 fusion.6
  94.8 7.0 all_gather.24
  101.8 62.7 %all-gather.7.cloned.1.call-done = bf16[1024,3584]{1,0:T(8,128)(2,1)} async-done(((bf16[1024,896]{1,0:T(8,128)(2,1)}), bf16[1024,3584]{1,0:T(8,128)(2,1)}) %all-gather.7.cloned.1.call-update) | async-done | bytes 7340048 | tf_op jit(solution)/shard_map/all_gather | solution.py:31
  164.5 4.7 fusion.3
  169.2 72.3 %all-gather.9.cloned.1.call-done = bf16[1024,3584]{1,0:T(8,128)(2,1)} async-done(((bf16[1024,896]{1,0:T(8,128)(2,1)}), bf16[1024,3584]{1,0:T(8,128)(2,1)}) %all-gather.9.cloned.1.call-update) | async-done | bytes 7340048 | tf_op jit(solution)/shard_map/all_gather | solution.py:32
  241.5 4.7 fusion.4
  246.2 2.9 pad_maximum_fusion
  249.2 74.3 %reduce-scatter.12.cloned.1.call-done = f32[24,3584]{1,0:T(8,128)} async-done(((f32[192,3584]{1,0:T(8,128)}), f32[24,3584]{1,0:T(8,128)}) %reduce-scatter.12.cloned.1.call-update) | async-done | bytes 344080 | tf_op jit(solution)/shard_map/reduce_scatter | solution.py:55
  323.5 96.8 %reduce-scatter.8.cloned.1.call-done = f32[24,7168]{1,0:T(8,128)} async-done(((f32[192,7168]{1,0:T(8,128)}), f32[24,7168]{1,0:T(8,128)}) %reduce-scatter.8.cloned.1.call-update) | async-done | bytes 688144 | tf_op jit(solution)/shard_map/reduce_scatter | solution.py:41
  420.3 2.1 multiply_convert_fusion
  422.6 0.7 all-gather.17.cloned.1.call-update
  424.1 47.0 %all-gather.15.cloned.1.call-done = bf16[192,3584]{1,0:T(8,128)(2,1)} async-done(((bf16[24,3584]{1,0:T(8,128)(2,1)}), bf16[192,3584]{1,0:T(8,128)(2,1)}) %all-gather.15.cloned.1.call-update) | async-done | bytes 1376272 | tf_op jit(solution)/shard_map/all_gather | solution.py:64
  471.1 6.4 fusion
  477.6 45.3 %all-gather.17.cloned.1.call-done = bf16[192,3584]{1,0:T(8,128)(2,1)} async-done(((bf16[24,3584]{1,0:T(8,128)(2,1)}), bf16[192,3584]{1,0:T(8,128)(2,1)}) %all-gather.17.cloned.1.call-update) | async-done | bytes 1376272 | tf_op jit(solution)/shard_map/all_gather | solution.py:65
  522.9 6.4 fusion.1
  529.3 45.3 %all-gather.11.cloned.1.call-done = bf16[192,3584]{1,0:T(8,128)(2,1)} async-done(((bf16[24,3584]{1,0:T(8,128)(2,1)}), bf16[192,3584]{1,0:T(8,128)(2,1)}) %all-gather.11.cloned.1.call-update) | async-done | bytes 1376272 | tf_op jit(solution)/shard_map/all_gather | solution.py:51
  574.6 6.5 convolution_convert_fusion
  581.4 1.1 copy-done
  582.4 5.6 fusion.7
  588.1 6.6 convolution_add_fusion
  594.8 5.7 fusion.5
  600.5 49.7 %reduce-scatter.16.cloned.1.call-done = bf16[1024,896]{0,1:T(8,128)(2,1)} async-done(((bf16[1024,3584]{0,1:T(8,128)(2,1)}), bf16[1024,896]{0,1:T(8,128)(2,1)}) %reduce-scatter.16.cloned.1.call-update) | async-done | bytes 1835024 | tf_op jit(solution)/shard_map/reduce_scatter | solution.py:74
  650.3 3.9 copy.10
  654.2 70.8 %reduce-scatter.18.cloned.1.call-done = bf16[1024,896]{0,1:T(8,128)(2,1)} async-done(((bf16[1024,3584]{0,1:T(8,128)(2,1)}), bf16[1024,896]{0,1:T(8,128)(2,1)}) %reduce-scatter.18.cloned.1.call-update) | async-done | bytes 1835024 | tf_op jit(solution)/shard_map/reduce_scatter | solution.py:80
  725.0 3.9 copy.11
  728.9 71.0 %reduce-scatter.20.cloned.1.call-done = bf16[896,1024]{1,0:T(8,128)(2,1)} async-done(((bf16[3584,1024]{1,0:T(8,128)(2,1)}), bf16[896,1024]{1,0:T(8,128)(2,1)}) %reduce-scatter.20.cloned.1.call-update) | async-done | bytes 1835024 | tf_op jit(solution)/shard_map/reduce_scatter | solution.py:86
  799.9 3.7 convert_element_type.49
  803.6 18.5 %reduce-scatter.14.cloned.1.call-done = f32[48,1024]{1,0:T(8,128)} async-done(((f32[192,1024]{1,0:T(8,128)}), f32[48,1024]{1,0:T(8,128)}) %reduce-scatter.14.cloned.1.call-update) | async-done | bytes 196624 | tf_op jit(solution)/shard_map/reduce_scatter | solution.py:67
  822.1 23.2 %reduce-scatter.10.cloned.1.call-done = f32[48,1024]{1,0:T(8,128)} async-done(((f32[192,1024]{1,0:T(8,128)}), f32[48,1024]{1,0:T(8,128)}) %reduce-scatter.10.cloned.1.call-update) | async-done | bytes 196624 | tf_op jit(solution)/shard_map/reduce_scatter | solution.py:53
  (33 shorter events, 2.9 us)
Async XLA Ops:
  7.2 2.3 copy-start.3
  7.2 80.3 %all-gather.13.cloned.1.call-start = ((), (), s32[]{:S(2)}) async-start(), calls=%async_computation.11 | async-start | bytes 9175040 | tf_op jit(solution)/shard_map/all_gather | solution.py:33
  7.9 156.6 %all-gather.7.cloned.1.call-start = ((), (), s32[]{:S(2)}) async-start(), calls=%async_computation.7 | async-start | bytes 9175040 | tf_op jit(solution)/shard_map/all_gather | solution.py:31
  8.7 232.9 %all-gather.9.cloned.1.call-start = ((), (), s32[]{:S(2)}) async-start(), calls=%async_computation.8 | async-start | bytes 9175040 | tf_op jit(solution)/shard_map/all_gather | solution.py:32
  9.4 314.1 %reduce-scatter.12.cloned.1.call-start = ((), (), s32[]{:S(2)}) async-start(), calls=%async_computation.13 | async-start | bytes 3096576 | tf_op jit(solution)/shard_map/reduce_scatter | solution.py:55
  17.3 77.4 %copy-start.4 = (bf16[48,1024]{1,0:T(8,128)(2,1)S(1)}, bf16[48,1024]{1,0:T(8,128)(2,1)}, u32[]{:S(2)}) copy-start(bf16[48,1024]{1,0:T(8,128)(2,1)} %param.5) | copy-start | bytes 294916
  94.7 325.6 %reduce-scatter.8.cloned.1.call-start = ((), (), s32[]{:S(2)}) async-start(), calls=%async_computation.9 | async-start | bytes 6193152 | tf_op jit(solution)/shard_map/reduce_scatter | solution.py:41
  249.1 222.0 %all-gather.15.cloned.1.call-start = ((), (), s32[]{:S(2)}) async-start(), calls=%async_computation.14 | async-start | bytes 1548288 | tf_op jit(solution)/shard_map/all_gather | solution.py:64
  422.5 100.4 %all-gather.17.cloned.1.call-start = ((), (), s32[]{:S(2)}) async-start(), calls=%async_computation.15 | async-start | bytes 1548288 | tf_op jit(solution)/shard_map/all_gather | solution.py:65
  423.3 151.4 %all-gather.11.cloned.1.call-start = ((), (), s32[]{:S(2)}) async-start(), calls=%async_computation.10 | async-start | bytes 1548288 | tf_op jit(solution)/shard_map/all_gather | solution.py:51
  424.0 226.3 %reduce-scatter.16.cloned.1.call-start = ((), (), s32[]{:S(2)}) async-start(), calls=%async_computation.17 | async-start | bytes 9175040 | tf_op jit(solution)/shard_map/reduce_scatter | solution.py:74
  477.5 247.5 %reduce-scatter.18.cloned.1.call-start = ((), (), s32[]{:S(2)}) async-start(), calls=%async_computation.18 | async-start | bytes 9175040 | tf_op jit(solution)/shard_map/reduce_scatter | solution.py:80
  529.3 270.6 %reduce-scatter.20.cloned.1.call-start = ((), (), s32[]{:S(2)}) async-start(), calls=%async_computation.19 | async-start | bytes 9175040 | tf_op jit(solution)/shard_map/reduce_scatter | solution.py:86
  581.1 1.3 copy-start
  581.1 6.9 copy-start.2
  581.1 241.0 %reduce-scatter.14.cloned.1.call-start = ((), (), s32[]{:S(2)}) async-start(), calls=%async_computation.16 | async-start | bytes 983040 | tf_op jit(solution)/shard_map/reduce_scatter | solution.py:67
  588.1 6.7 copy-start.1
  594.7 250.5 %reduce-scatter.10.cloned.1.call-start = ((), (), s32[]{:S(2)}) async-start(), calls=%async_computation.12 | async-start | bytes 983040 | tf_op jit(solution)/shard_map/reduce_scatter | solution.py:53
Sparse Core Ops, SparseCore 0:
  9.7 77.7 all-gather.12
  89.2 75.2 all-gather.6
  166.2 75.2 all-gather.8
  245.8 77.6 reduce-scatter.11
  327.3 92.9 reduce-scatter.7
  423.4 47.6 all-gather.14
  474.2 48.5 all-gather.16
  526.0 48.5 all-gather.10
  577.2 73.0 reduce-scatter.15
  652.6 72.3 reduce-scatter.17
  727.5 72.3 reduce-scatter.19
  802.9 19.1 reduce-scatter.13
  825.2 20.0 reduce-scatter.9
where the time goes:
time: 852 us
  waiting for transfers between devices  751 us (88%)
  matrix products  53.8 us (6%)
  blocking collectives  14.9 us (2%)
  between operations  14 us (2%)
  local copies, waits for them, and re-layouts  8.93 us (1%)
  other arithmetic  8.77 us (1%)
    reduce_scatter x1, waiting for transfers between devices, body(): lax.psum_scatter(jnp.concatenate([product(segment, gate_panel), product(s...  96.8 us
    reduce_scatter x1, waiting for transfers between devices, body(): lax.psum_scatter(product_transposed(segment, down_panel), 'row', scatter_...  74.3 us
    all_gather x1, waiting for transfers between devices, body(): lax.all_gather(up_weight, 'depth', axis=1, tiled=True)  72.3 us
    reduce_scatter x1, waiting for transfers between devices, body(): lax.psum_scatter(rounded_partial(hidden_all, cotangent_all).astype(jnp.bf...  71 us
    reduce_scatter x1, waiting for transfers between devices, body(): lax.psum_scatter(rounded_partial(token_all, up_grad_all).astype(jnp.bfloa...  70.8 us
    all_gather x1, waiting for transfers between devices, body(): lax.all_gather(down_weight, 'depth', axis=0, tiled=True)  70.2 us
    all_gather x1, waiting for transfers between devices, body(): lax.all_gather(gate_weight, 'depth', axis=1, tiled=True)  62.7 us
    reduce_scatter x1, waiting for transfers between devices, body(): lax.psum_scatter(rounded_partial(token_all, gate_grad_all).astype(jnp.bfl...  49.7 us
  transfers between devices with their start and end apart: 13, of which 13 were waited for; matrix products, arithmetic and copies ran while one was open for 8% of the time, Pallas kernels for 0%

commit v1 on v0

v1 whole, which is shorter than its diff:
```python
import functools

import jax
import jax.numpy as jnp
from jax import lax
from jax.experimental import pallas as pl
from jax.experimental.pallas import tpu as pltpu
from jax.sharding import PartitionSpec as P

MESH = pl.DeviceIdType.MESH
BF = jnp.bfloat16
F32 = jnp.float32
OFFSETS = (0, 2, 1, 3)
B = 48
D = 1024
F = 896
CUT = 512


def dot(a, b):
    return jnp.dot(a, b, preferred_element_type=F32)


def dot_t(a, b):
    return lax.dot_general(a, b, (((1,), (1,)), ((), ())), preferred_element_type=F32)


def kernel(tok_in, cot_in, gw_in, uw_in, dw_in,
           mixed_out, tg_out, buf_out, all_out,
           buf, gw, uw, dw, part0, part1, r0y, s0, r0x, r1x, s1, r1y, all0, all1, pk, sk, ps, pr,
           w_sem, l_sem, o_sem, p1s, p1r, fs, fr,
           s0y_s, s0y_r, s0x_s, s0x_r, s1x_s, s1x_r, s1y_s, s1y_r,
           g0x_s, g0x_r, g0y_s, g0y_r, g1y_s, g1y_r, g1x_s, g1x_r,
           ks, kr, p4s, p4r):
    row, col, z = lax.axis_index("row"), lax.axis_index("col"), lax.axis_index("depth")
    x, yh = row // 2, row % 2
    yl, k = col // 2, col % 2

    sibling = (row, yl * 2 + (1 - k), z)
    y_peer = (x * 2 + (1 - yh), col, z)

    def x_at(dx):
        return (x + dx) % 4

    def x_peer(dx):
        return (x_at(dx) * 2 + yh, col, z)

    def plane_peer(dz, dyl):
        return (row, ((yl + dyl) % 2) * 2 + k, (z + dz) % 4)

    others = [(t, dyl) for t in range(4) for dyl in range(2) if (t, dyl) != (0, 0)]
    sends = []

    def remote(src, dst, ssem, rsem, dev):
        cp = pltpu.make_async_remote_copy(src_ref=src, dst_ref=dst, send_sem=ssem, recv_sem=rsem,
                                          device_id=dev, device_id_type=MESH)
        cp.start()
        sends.append(cp)
        return cp

    weights = [pltpu.make_async_copy(a, b, w_sem.at[i])
               for i, (a, b) in enumerate(((gw_in, gw), (uw_in, uw), (dw_in, dw)))]
    own = [pltpu.make_async_copy(a, buf.at[i, col], l_sem.at[i]) for i, a in enumerate((tok_in, cot_in))]
    for cp in own + weights:
        cp.start()

    barrier = pltpu.get_barrier_semaphore()
    peers = [sibling, y_peer] + [x_peer(dx) for dx in (1, 2, 3)]
    peers += [plane_peer(OFFSETS[t], dyl) for t, dyl in others]
    for dev in peers:
        pl.semaphore_signal(barrier, inc=1, device_id=dev, device_id_type=MESH)
    pl.semaphore_wait(barrier, len(peers))
    for cp in own:
        cp.wait()

    arrived, handed = {}, {}

    def share(t, dyl):
        i = t * 2 + dyl
        arrived[i] = remote(buf.at[:, col], buf.at[:, t * 4 + col], p1s.at[i], p1r.at[i],
                            plane_peer(-OFFSETS[t], dyl))

    def hand_on(t, dyl):
        i = t * 2 + dyl
        slot = t * 4 + ((yl + dyl) % 2) * 2 + k
        handed[i] = remote(buf.at[:, slot], buf.at[:, slot], fs.at[i], fr.at[i], sibling)

    def take(half):
        for t in (2 * half, 2 * half + 1):
            for dyl in range(2):
                if t or dyl:
                    arrived[t * 2 + dyl].wait_recv()
                    hand_on(t, dyl)

    def ready(half):
        for i in range(4 * half, 4 * half + 4):
            handed[i].wait_recv()

    for t, dyl in ((0, 1), (1, 0), (1, 1)):
        share(t, dyl)
    hand_on(0, 0)

    def partial(half, dst, lo, width):
        rows = [buf[a, 8 * half:8 * half + 8].reshape(8 * B, D) for a in range(2)]
        cols = slice(lo, lo + width)
        for i, value in enumerate((lambda: dot(rows[0], gw[:, cols]), lambda: dot(rows[0], uw[:, cols]),
                                   lambda: dot_t(rows[1], dw[cols, :]))):
            dst[half, i] = value().astype(BF).reshape(8, B, width)

    rs0y, rs1x, rs0x, rs1y = {}, {}, {}, {}

    def send0y(h):
        rs0y[h] = remote(part0.at[h, :, pl.ds((1 - yh) * 4, 4)], r0y.at[h], s0y_s.at[h], s0y_r.at[h], y_peer)

    def send1x(h):
        rs1x[h] = [remote(part1.at[h, :, pl.ds(x_at(dx) * 2, 2)], r1x.at[h, dx - 1],
                          s1x_s.at[h, dx - 1], s1x_r.at[h, dx - 1], x_peer(dx)) for dx in (1, 2, 3)]

    def send0x(h):
        rs0y[h].wait_recv()
        s0[h] = (part0[h, :, pl.ds(yh * 4, 4)].astype(F32) + r0y[h].astype(F32)).astype(BF)
        rs0x[h] = [remote(s0.at[h, :, x_at(dx)], r0x.at[h, dx - 1],
                          s0x_s.at[h, dx - 1], s0x_r.at[h, dx - 1], x_peer(dx)) for dx in (1, 2, 3)]

    def send1y(h):
        for cp in rs1x[h]:
            cp.wait_recv()
        total = part1[h, :, pl.ds(x * 2, 2)].astype(F32)
        for i in range(3):
            total = total + r1x[h, i].astype(F32)
        s1[h] = total.astype(BF)
        rs1y[h] = remote(s1.at[h, :, 1 - yh], r1y.at[h], s1y_s.at[h], s1y_r.at[h], y_peer)

    def activate(total, dst, slot):
        gate, up, hidden_grad = total[0], total[1], total[2]
        sigma = jax.nn.sigmoid(gate)
        activated = gate * sigma
        dst[0, slot] = (activated * up).astype(BF)
        dst[1, slot] = (hidden_grad * up * sigma * (1.0 + gate * (1.0 - sigma))).astype(BF)
        dst[2, slot] = (hidden_grad * activated).astype(BF)

    ag0x, ag0y, ag1y, ag1x = {}, {}, {}, {}

    def gather0x(h):
        for cp in rs0x[h]:
            cp.wait_recv()
        total = s0[h, :, x].astype(F32)
        for i in range(3):
            total = total + r0x[h, i].astype(F32)
        slot = h * 8 + yh * 4 + x
        activate(total, all0, slot)
        ag0x[h] = [remote(all0.at[:, slot], all0.at[:, slot], g0x_s.at[h, dx - 1], g0x_r.at[h, dx - 1], x_peer(dx))
                   for dx in (1, 2, 3)]

    def gather1y(h):
        rs1y[h].wait_recv()
        total = s1[h, :, yh].astype(F32) + r1y[h].astype(F32)
        slot = h * 8 + x * 2 + yh
        activate(total, all1, slot)
        ag1y[h] = remote(all1.at[:, slot], all1.at[:, slot], g1y_s.at[h], g1y_r.at[h], y_peer)

    def gather0y(h):
        for cp in ag0x[h]:
            cp.wait_recv()
        slots = pl.ds(h * 8 + yh * 4, 4)
        ag0y[h] = remote(all0.at[:, slots], all0.at[:, slots], g0y_s.at[h], g0y_r.at[h], y_peer)

    def gather1x(h):
        ag1y[h].wait_recv()
        slots = pl.ds(h * 8 + x * 2, 2)
        ag1x[h] = [remote(all1.at[:, slots], all1.at[:, slots], g1x_s.at[h, dx - 1], g1x_r.at[h, dx - 1], x_peer(dx))
                   for dx in (1, 2, 3)]

    pair = {}

    def outputs(h):
        ag0y[h].wait_recv()
        for cp in ag1x[h]:
            cp.wait_recv()
        rows = slice(8 * h, 8 * h + 8)
        left = [(all0[i, rows].reshape(8 * B, CUT), all1[i, rows].reshape(8 * B, F - CUT)) for i in range(3)]
        for n in range(2):
            cols = slice(n * 512, n * 512 + 512)
            mixed = dot(left[0][0], dw[:CUT, cols]) + dot(left[0][1], dw[CUT:, cols])
            grad = (dot_t(left[1][0], gw[cols, :CUT]) + dot_t(left[1][1], gw[cols, CUT:])
                    + dot_t(left[2][0], uw[cols, :CUT]) + dot_t(left[2][1], uw[cols, CUT:]))
            for a, value in enumerate((mixed, grad)):
                value = value.astype(BF).reshape(4, 2, B, 512)
                for core in range(2):
                    pk[core, a, 4 * h:4 * h + 4, :, cols] = value[:, core]
        half = pl.ds(4 * h, 4)
        pair[h] = remote(pk.at[1 - k, :, half], sk.at[:, half], ks.at[h], kr.at[h], sibling)

    spread = {}

    def reduce(h):
        pair[h].wait_recv()
        half = slice(4 * h, 4 * h + 4)
        ps[:, half] = (pk[k, :, half].astype(F32) + sk[:, half].astype(F32)).astype(BF)
        for t in (2 * h, 2 * h + 1):
            for dyl in range(2):
                if t or dyl:
                    i = t * 2 + dyl
                    spread[i] = remote(ps.at[:, t * 2 + (yl + dyl) % 2], pr.at[i], p4s.at[i], p4r.at[i],
                                       plane_peer(OFFSETS[t], dyl))

    take(0)
    for t, dyl in ((2, 0), (3, 0), (2, 1), (3, 1)):
        share(t, dyl)
    for cp in weights:
        cp.wait()
    ready(0)
    partial(0, part0, 0, CUT)
    send0y(0)
    partial(0, part1, CUT, F - CUT)
    send1x(0)
    take(1)
    ready(1)
    partial(1, part0, 0, CUT)
    send0y(1)
    partial(1, part1, CUT, F - CUT)
    send1x(1)
    send1y(0)
    send0x(0)
    gather1y(0)
    gather0x(0)
    gather1x(0)
    gather0y(0)
    send1y(1)
    send0x(1)
    gather1y(1)
    gather0x(1)
    gather1x(1)
    gather0y(1)
    outputs(0)
    reduce(0)
    outputs(1)
    reduce(1)

    results = [pltpu.make_async_copy(buf, buf_out, o_sem.at[0]),
               pltpu.make_async_copy(all0, all_out.at[:, :, :, pl.ds(0, CUT)], o_sem.at[1]),
               pltpu.make_async_copy(all1, all_out.at[:, :, :, pl.ds(CUT, F - CUT)], o_sem.at[2])]
    for cp in results:
        cp.start()

    total = ps[:, yl].astype(F32)
    for t, dyl in others:
        i = t * 2 + dyl
        spread[i].wait_recv()
        total = total + pr[i].astype(F32)
    mixed_out[...] = total[0]
    tg_out[...] = total[1]
    for cp in sends:
        cp.wait_send()
    for cp in results:
        cp.wait()


def body(tokens, gate_weight, up_weight, down_weight, cotangent):
    dma = pltpu.SemaphoreType.DMA
    vmem = lambda *shape: pltpu.VMEM(shape, BF)
    whole = pl.BlockSpec(memory_space=pl.ANY)
    G = F - CUT
    mixed, token_grad, rows, hidden = pl.pallas_call(
        kernel,
        out_shape=(
            jax.ShapeDtypeStruct((B, D), F32),
            jax.ShapeDtypeStruct((B, D), F32),
            jax.ShapeDtypeStruct((2, 16, B, D), BF),
            jax.ShapeDtypeStruct((3, 16, B, F), BF),
        ),
        in_specs=[whole] * 5,
        out_specs=(pl.BlockSpec(memory_space=pltpu.VMEM),) * 2 + (whole,) * 2,
        scratch_shapes=[
            vmem(2, 16, B, D), vmem(D, F), vmem(D, F), vmem(F, D),
            vmem(2, 3, 8, B, CUT), vmem(2, 3, 8, B, G),
            vmem(2, 3, 4, B, CUT), vmem(2, 3, 4, B, CUT), vmem(2, 3, 3, B, CUT),
            vmem(2, 3, 3, 2, B, G), vmem(2, 3, 2, B, G), vmem(2, 3, B, G),
            vmem(3, 16, B, CUT), vmem(3, 16, B, G),
            vmem(2, 2, 8, B, D), vmem(2, 8, B, D), vmem(2, 8, B, D), vmem(8, 2, B, D),
            dma((3,)), dma((2,)), dma((3,)), dma((8,)), dma((8,)), dma((8,)), dma((8,)),
            dma((2,)), dma((2,)), dma((2, 3)), dma((2, 3)), dma((2, 3)), dma((2, 3)), dma((2,)), dma((2,)),
            dma((2, 3)), dma((2, 3)), dma((2,)), dma((2,)), dma((2,)), dma((2,)), dma((2, 3)), dma((2, 3)),
            dma((2,)), dma((2,)), dma((8,)), dma((8,)),
        ],
        compiler_params=pltpu.CompilerParams(
            collective_id=0, has_side_effects=True, vmem_limit_bytes=60 * 2**20
        ),
    )(tokens, cotangent, gate_weight, up_weight, down_weight)
    tokens_all, cotangent_all = rows[0].reshape(16 * B, D), rows[1].reshape(16 * B, D)
    hidden_all, gate_grad, up_grad = (hidden[i].reshape(16 * B, F) for i in range(3))

    def over_tokens(left, right):
        return lax.dot_general(left, right, (((0,), (0,)), ((), ())), preferred_element_type=F32)

    return (mixed, token_grad, over_tokens(tokens_all, gate_grad), over_tokens(tokens_all, up_grad),
            over_tokens(hidden_all, cotangent_all))


def solution(mesh):
    placed = (
        P(("depth", "col"), "row"),
        P("row", ("col", "depth")),
        P("row", ("col", "depth")),
        P(("col", "depth"), "row"),
        P(("depth", "col"), "row"),
    )
    return jax.shard_map(
        body,
        mesh=mesh,
        in_specs=placed,
        out_specs=(
            P(("depth", "col"), "row"),
            P(("depth", "col"), "row"),
            P("row", ("col", "depth")),
            P("row", ("col", "depth")),
            P(("col", "depth"), "row"),
        ),
        check_vma=False,
    )
```

time: 852 us -> 135 us (0.16)
  waiting for transfers between devices: 751 us -> 0 us
  Pallas kernels: 0 us -> 120 us
  matrix products: 53.8 us -> 12.8 us
  blocking collectives: 14.9 us -> 0 us
  between operations: 14 us -> 0.66 us
  other arithmetic: 8.77 us -> 0 us
    reduce_scatter x7 -> x0, waiting for transfers between devices: 404 us -> none  [the longest x1 96.8 us: body(): lax.psum_scatter(jnp.concatenate([product(segment, gate_panel), product(s...]
    all_gather x6 -> x0, waiting for transfers between devices: 343 us -> none  [the longest x1 72.3 us: body(): lax.all_gather(up_weight, 'depth', axis=1, tiled=True)]
    pallas_call x0 -> x1, Pallas kernels: none -> 120 us  [body(): pl.pallas_call(kernel, out_shape=(jax.ShapeDtypeStruct((B, D), F32), jax....]
    dot_general x9 -> x3, matrix products: 53.8 us -> 12.8 us  [over_tokens(): lax.dot_general(left, right, (((0,), (0,)), ((), ())), preferred_element_...]
    all_gather x2 -> x0, blocking collectives: 14.9 us -> none  [the longest x1 7.88 us: body(): lax.all_gather(cotangent, 'col', axis=0, tiled=True)]
  transfers between devices with their start and end apart: 13 -> 0, of which waited for: 13 -> 0; matrix products, arithmetic and copies ran while one was open for 8% -> 0% of each run, Pallas kernels for 0% -> 0%
where the time goes in v1:
time: 135 us
  Pallas kernels  120 us (89%)
  matrix products  12.8 us (9%)
  local copies, waits for them, and re-layouts  1.37 us (1%)
    pallas_call x1, Pallas kernels, body(): pl.pallas_call(kernel, out_shape=(jax.ShapeDtypeStruct((B, D), F32), jax....  120 us
    dot_general x3, matrix products, over_tokens(): lax.dot_general(left, right, (((0,), (0,)), ((), ())), preferred_element_...  12.8 us

profile of v1, /device:TPU:1, one launch (start us, length us, event | category | flops | bytes accessed | tf_op | source)
XLA Modules:
  0.0 134.5 jit_solution(4899456726841722312)
XLA Ops:
  0.6 119.7 %shard_map.92 = (f32[48,1024]{1,0:T(8,128)}, f32[48,1024]{1,0:T(8,128)}, bf16[2,16,48,1024]{3,2,1,0:T(8,128)(2,1)}, bf16[3,16,48,896]{3,2,1,0:T(8,128)(2,1)}) custom-call(bf16[48,1024]{1,0:T(8,128)(2,1)} %tok_in.1, bf16[48,1024]{1,0:T(8,128)(2,1)} %cot_in.1, bf16[1024,896]{1,0:T(8,128)(2,1)} %gw_in.1, bf16[1024,896]{1,0:T(8,128)(2,1)} %uw_in.1, ...), custom_call_target="tpu_custom_call" | custom-call | tf_op jit(solution)/shard_map/pallas_call | solution.py:264
  120.3 0.0 copy-start.2
  120.3 0.0 copy-start.3
  120.4 5.6 %convolution_bitcast_fusion.1 = f32[1024,896]{1,0:T(8,128)} fusion(bf16[2,16,48,1024]{3,2,1,0:T(8,128)(2,1)} %get-tuple-element.11, bf16[3,16,48,896]{3,2,1,0:T(8,128)(2,1)} %get-tuple-element.12), kind=kOutput, calls=%fused_computation.1 | convolution fusion | flops 1409286144 | bytes 6619136 | tf_op jit(solution)/shard_map/dot_general | solution.py:294
  126.0 0.0 copy-done.2
  126.0 0.0 copy-done.3
  126.0 3.5 %convolution_bitcast_fusion = f32[896,1024]{1,0:T(8,128)} fusion(bf16[2,16,48,1024]{3,2,1,0:T(8,128)(2,1)S(1)} %copy-done.3, bf16[3,16,48,896]{3,2,1,0:T(8,128)(2,1)S(1)} %copy-done.2), kind=kOutput, calls=%fused_computation | convolution fusion | flops 1409286144 | bytes 6619136 | tf_op jit(solution)/shard_map/dot_general | solution.py:294
  129.5 0.0 copy-start.1
  129.5 0.0 copy-start
  129.5 3.7 %convolution_bitcast_fusion.2 = f32[1024,896]{1,0:T(8,128)} fusion(bf16[2,16,48,1024]{3,2,1,0:T(8,128)(2,1)S(1)} %copy-done.3, bf16[3,16,48,896]{3,2,1,0:T(8,128)(2,1)S(1)} %copy-done.2), kind=kOutput, calls=%fused_computation.2 | convolution fusion | flops 1409286144 | bytes 6619136 | tf_op jit(solution)/shard_map/dot_general | solution.py:294
  133.2 0.0 copy-done.1
  133.2 0.7 copy.12
  133.9 0.0 copy-done
  133.9 0.7 copy.13
Async XLA Ops:
  120.3 5.7 %copy-start.2 = (bf16[3,16,48,896]{3,2,1,0:T(8,128)(2,1)S(1)}, bf16[3,16,48,896]{3,2,1,0:T(8,128)(2,1)}, u32[]{:S(2)}) copy-start(bf16[3,16,48,896]{3,2,1,0:T(8,128)(2,1)} %get-tuple-element.12) | copy-start | bytes 12386308
  120.3 5.7 %copy-start.3 = (bf16[2,16,48,1024]{3,2,1,0:T(8,128)(2,1)S(1)}, bf16[2,16,48,1024]{3,2,1,0:T(8,128)(2,1)}, u32[]{:S(2)}) copy-start(bf16[2,16,48,1024]{3,2,1,0:T(8,128)(2,1)} %get-tuple-element.11) | copy-start | bytes 9437188
  129.5 3.7 %copy-start.1 = (f32[48,1024]{1,0:T(8,128)S(1)}, f32[48,1024]{1,0:T(8,128)}, u32[]{:S(2)}) copy-start(f32[48,1024]{1,0:T(8,128)} %get-tuple-element.18) | copy-start | bytes 589828
  129.5 4.4 %copy-start = (f32[48,1024]{1,0:T(8,128)S(1)}, f32[48,1024]{1,0:T(8,128)}, u32[]{:S(2)}) copy-start(f32[48,1024]{1,0:T(8,128)} %get-tuple-element.19) | copy-start | bytes 589828

commit v2 on v0

v2 whole, which is shorter than its diff:
```python
import functools

import jax
import jax.numpy as jnp
from jax import lax
from jax.experimental import pallas as pl
from jax.experimental.pallas import tpu as pltpu
from jax.sharding import PartitionSpec as P

MESH = pl.DeviceIdType.MESH
BF = jnp.bfloat16
F32 = jnp.float32
OFFSETS = (0, 2, 1, 3)
B = 48
D = 1024
F = 896
CUT = 512
G = F - CUT
PIECE = 256


def dot(a, b):
    return jnp.dot(a, b, preferred_element_type=F32)


def dot_t(a, b):
    return lax.dot_general(a, b, (((1,), (1,)), ((), ())), preferred_element_type=F32)


def dot_rows(a, b):
    return lax.dot_general(a, b, (((0,), (0,)), ((), ())), preferred_element_type=F32)


def kernel(tok_in, cot_in, gw_in, uw_in, dw_in,
           mixed_out, tg_out, gate_out, up_out, down_out,
           buf, gw, uw, dw, part0, part1, xa, xd, xc, s0, r0y, y1, s1, ya, yb, all0, all1,
           pk, sk, ps, pz, pq, py, pr, gate_acc, up_acc, down_acc,
           w_sem, l_sem, p1s, p1r, fs, fr,
           xa_s, xa_r, xd_s, xd_r, xc_s, xc_r, r0y_s, r0y_r, y1_s, y1_r, ya_s, ya_r, yb_s, yb_r,
           g0y_s, g0y_r, g0x_s, g0x_r, g0f_s, g0f_r, g1x_s, g1x_r, g1f_s, g1f_r, g1y_s, g1y_r,
           ks, kr, p4s, p4r):
    row, col, z = lax.axis_index("row"), lax.axis_index("col"), lax.axis_index("depth")
    x, yh = row // 2, row % 2
    yl, k = col // 2, col % 2
    turn = 1 - 2 * k
    mate = (1 - yl) * 2 + k

    sibling = (row, yl * 2 + (1 - k), z)
    y_peer = (x * 2 + (1 - yh), col, z)
    lo_peer = (row, mate, z)

    def x_at(dx):
        return (x + dx + 8) % 4

    def x_peer(dx):
        return (x_at(dx) * 2 + yh, col, z)

    def plane_peer(dz, dyl):
        return (row, ((yl + dyl) % 2) * 2 + k, (z + dz) % 4)

    others = [(t, dyl) for t in range(4) for dyl in range(2) if (t, dyl) != (0, 0)]
    sends = []

    def remote(src, dst, ssem, rsem, dev):
        cp = pltpu.make_async_remote_copy(src_ref=src, dst_ref=dst, send_sem=ssem, recv_sem=rsem,
                                          device_id=dev, device_id_type=MESH)
        cp.start()
        sends.append(cp)
        return cp

    weights = [pltpu.make_async_copy(a, b, w_sem.at[i])
               for i, (a, b) in enumerate(((gw_in, gw), (uw_in, uw), (dw_in, dw)))]
    own = [pltpu.make_async_copy(a, buf.at[i, col], l_sem.at[i]) for i, a in enumerate((tok_in, cot_in))]
    for cp in own + weights:
        cp.start()

    barrier = pltpu.get_barrier_semaphore()
    peers = [sibling, y_peer] + [x_peer(dx) for dx in (1, 3)]
    peers += [plane_peer(OFFSETS[t], dyl) for t, dyl in others]
    for dev in peers:
        pl.semaphore_signal(barrier, inc=1, device_id=dev, device_id_type=MESH)
    pl.semaphore_wait(barrier, len(peers))

    moved, handed = {}, {}

    def share(name, a, i, src, dst, dev):
        moved[name, a] = remote(buf.at[a, src], buf.at[a, dst], p1s.at[a, i], p1r.at[a, i], dev)

    def hand_on(a, i, slot):
        handed[a, i] = remote(buf.at[a, slot], buf.at[a, slot], fs.at[a, i], fr.at[a, i], sibling)

    def spread_first():
        for a in range(2):
            own[a].wait()
            share("lo", a, 0, col, col, lo_peer)
            share("far", a, 1, col, 4 + col, plane_peer(2, 0))
            hand_on(a, 0, col)
        for a in range(2):
            moved["lo", a].wait_recv()
            hand_on(a, 1, mate)
            moved["far", a].wait_recv()
            share("far_lo", a, 6, 4 + col, 4 + col, lo_peer)
            hand_on(a, 2, 4 + col)
            for i, (t, slot) in enumerate(((2, col), (3, col), (2, mate), (3, mate))):
                share((t, i // 2), a, 2 + i, slot, 4 * t + slot, plane_peer(-OFFSETS[t], 0))

    def spread_last(a):
        moved["far_lo", a].wait_recv()
        hand_on(a, 3, 4 + mate)

    def spread_second(a):
        for i, slot in enumerate((col, mate)):
            for t in (2, 3):
                moved[(t, i), a].wait_recv()
                hand_on(a, 2 * t + i, 4 * t + slot)

    def ready(h, a):
        for i in range(4 * h, 4 * h + 4):
            handed[a, i].wait_recv()

    def tokens_part(h, dst, lo, width):
        rows = buf[0, 8 * h:8 * h + 8].reshape(8 * B, D)
        for i, weight in enumerate((gw, uw)):
            dst[h, i] = dot(rows, weight[:, lo:lo + width]).astype(BF).reshape(8, B, width)

    def cotangent_part(h, dst, lo, width):
        rows = buf[1, 8 * h:8 * h + 8].reshape(8 * B, D)
        dst[h, 2] = dot_t(rows, dw[lo:lo + width, :]).astype(BF).reshape(8, B, width)

    def activate(total, dst, slot):
        gate, up, hidden_grad = total[0], total[1], total[2]
        sigma = jax.nn.sigmoid(gate)
        activated = gate * sigma
        dst[0, slot] = (activated * up).astype(BF)
        dst[1, slot] = (hidden_grad * up * sigma * (1.0 + gate * (1.0 - sigma))).astype(BF)
        dst[2, slot] = (hidden_grad * activated).astype(BF)

    cxa, cxd, cxc, cr0 = {}, {}, {}, {}

    def x_tokens(h):
        tokens_part(h, part0, 0, CUT)

    def x_first(h):
        cotangent_part(h, part0, 0, CUT)
        cxa[h] = [remote(part0.at[h, :, x_at(2) * 2 + i], xa.at[h, i], xa_s.at[h, i], xa_r.at[h, i], x_peer(1 - 2 * i))
                  for i in range(2)]
        cxd[h] = [remote(part0.at[h, :, x_at(1 - 2 * i) * 2 + 1 - i], xd.at[h, i], xd_s.at[h, i], xd_r.at[h, i],
                         x_peer(1 - 2 * i)) for i in range(2)]

    def x_second(h):
        cxc[h] = []
        for i in range(2):
            cxa[h][i].wait_recv()
            xa[h, i] = (xa[h, i].astype(F32) + part0[h, :, x_at(1 - 2 * i) * 2 + i].astype(F32)).astype(BF)
            cxc[h].append(remote(xa.at[h, i], xc.at[h, i], xc_s.at[h, i], xc_r.at[h, i], x_peer(1 - 2 * i)))

    def x_third(h):
        for cp in cxd[h] + cxc[h]:
            cp.wait_recv()
        for i in range(2):
            s0[h, :, i] = (part0[h, :, x * 2 + i].astype(F32) + xd[h, 1 - i].astype(F32)
                           + xc[h, i].astype(F32)).astype(BF)
        cr0[h] = remote(s0.at[h, :, 1 - yh], r0y.at[h], r0y_s.at[h], r0y_r.at[h], y_peer)

    cy1, cya, cyb = {}, {}, {}

    def y_first(h):
        tokens_part(h, part1, CUT, G)
        cotangent_part(h, part1, CUT, G)
        cy1[h] = {j: remote(part1.at[h, :, (1 - yh) * 4 + x_at(turn * j)], y1.at[h, j], y1_s.at[h, j], y1_r.at[h, j],
                            y_peer) for j in (2, 1, 3, 0)}
        cya[h], cyb[h] = {}, {}

    def lap(h, kind, src, ways):
        if "a" in ways:
            cya[h][kind] = remote(src.at[:, :, pl.ds(0, PIECE)], ya.at[h, kind], ya_s.at[h, kind], ya_r.at[h, kind],
                                  x_peer(turn if kind != 1 else -turn))
        if "b" in ways:
            cyb[h][kind] = remote(src.at[:, :, pl.ds(PIECE, G - PIECE)], yb.at[h, kind], yb_s.at[h, kind],
                                  yb_r.at[h, kind], x_peer(-turn if kind != 1 else turn))

    def y_second(h):
        for j in (2, 1, 3, 0):
            cy1[h][j].wait_recv()
            s1[h, j] = (part1[h, :, yh * 4 + x_at(turn * j)].astype(F32) + y1[h, j].astype(F32)).astype(BF)
            if j == 2:
                lap(h, 0, s1.at[h, 2], "ab")
            elif j == 1:
                lap(h, 1, s1.at[h, 1], "b")
            elif j == 3:
                lap(h, 1, s1.at[h, 3], "a")

    def y_third(h):
        cya[h][0].wait_recv()
        s1[h, 1, :, :, :PIECE] = (s1[h, 1, :, :, :PIECE].astype(F32) + ya[h, 0].astype(F32)).astype(BF)
        lap(h, 2, s1.at[h, 1], "a")
        cyb[h][0].wait_recv()
        s1[h, 3, :, :, PIECE:] = (s1[h, 3, :, :, PIECE:].astype(F32) + yb[h, 0].astype(F32)).astype(BF)
        lap(h, 2, s1.at[h, 3], "b")

    cg0y, cg0x, cg0f, cg1x, cg1f, cg1y = {}, {}, {}, {}, {}, {}

    def gather0(h, slot, kind):
        for i in range(2):
            cg0x[h, i, kind] = remote(all0.at[:, slot], all0.at[:, slot], g0x_s.at[h, i, kind], g0x_r.at[h, i, kind],
                                      x_peer(1 - 2 * i))

    def x_gather(h):
        cr0[h].wait_recv()
        slot = h * 8 + x * 2 + yh
        activate(s0[h, :, yh].astype(F32) + r0y[h].astype(F32), all0, slot)
        cg0y[h] = remote(all0.at[:, slot], all0.at[:, slot], g0y_s.at[h], g0y_r.at[h], y_peer)
        gather0(h, slot, 0)

    def x_gather_second(h):
        cg0y[h].wait_recv()
        gather0(h, h * 8 + x * 2 + 1 - yh, 1)

    def x_forward(h):
        for i, slot in enumerate((h * 8 + x_at(-1) * 2 + yh, h * 8 + x_at(1) * 2 + 1 - yh)):
            cg0x[h, i, i].wait_recv()
            cg0f[h, i] = remote(all0.at[:, slot], all0.at[:, slot], g0f_s.at[h, i], g0f_r.at[h, i], x_peer(1 - 2 * i))

    def x_done(h):
        for cp in (cg0x[h, 0, 1], cg0x[h, 1, 0], cg0f[h, 0], cg0f[h, 1]):
            cp.wait_recv()

    def to_y(h, j, slot):
        cg1y[h, j] = remote(all1.at[:, slot], all1.at[:, slot], g1y_s.at[h, j], g1y_r.at[h, j], y_peer)

    def y_gather(h):
        for cp in (cya[h][1], cya[h][2], cyb[h][1], cyb[h][2]):
            cp.wait_recv()
        mine = s1[h, 0].astype(F32)
        left = mine[:, :, :PIECE] + ya[h, 1].astype(F32) + ya[h, 2].astype(F32)
        right = mine[:, :, PIECE:] + yb[h, 1].astype(F32) + yb[h, 2].astype(F32)
        slot = h * 8 + yh * 4 + x
        activate(jnp.concatenate([left, right], axis=2), all1, slot)
        for i in range(2):
            cg1x[h, i] = remote(all1.at[:, slot], all1.at[:, slot], g1x_s.at[h, i], g1x_r.at[h, i],
                                x_peer(turn * (1 - 2 * i)))
        to_y(h, 0, slot)

    def y_forward(h):
        for i, (lo, width) in enumerate(((0, PIECE), (PIECE, G - PIECE))):
            slot = h * 8 + yh * 4 + x_at(turn * (2 * i - 1))
            cg1x[h, i].wait_recv()
            piece = all1.at[:, slot, :, pl.ds(lo, width)]
            cg1f[h, i] = remote(piece, piece, g1f_s.at[h, i], g1f_r.at[h, i], x_peer(turn * (1 - 2 * i)))
            to_y(h, 3 - 2 * i, slot)

    def y_forward_last(h):
        for i in range(2):
            cg1f[h, i].wait_recv()
        to_y(h, 2, h * 8 + yh * 4 + x_at(2))

    def y_done(h):
        for j in range(4):
            cg1y[h, j].wait_recv()

    pair = {}

    def output(h, a):
        rows = slice(8 * h, 8 * h + 8)
        which = (0,) if a == 0 else (1, 2)
        left = {i: (all0[i, rows].reshape(8 * B, CUT), all1[i, rows].reshape(8 * B, G)) for i in which}
        for n in range(2):
            cols = slice(n * 512, n * 512 + 512)
            if a == 0:
                value = dot(left[0][0], dw[:CUT, cols]) + dot(left[0][1], dw[CUT:, cols])
            else:
                value = (dot_t(left[1][0], gw[cols, :CUT]) + dot_t(left[1][1], gw[cols, CUT:])
                         + dot_t(left[2][0], uw[cols, :CUT]) + dot_t(left[2][1], uw[cols, CUT:]))
            value = value.astype(BF).reshape(4, 2, B, 512)
            for core in range(2):
                pk[core, a, 4 * h:4 * h + 4, :, cols] = value[:, core]
        half = pl.ds(4 * h, 4)
        pair[h, a] = remote(pk.at[1 - k, a, half], sk.at[a, half], ks.at[h, a], kr.at[h, a], sibling)

    def outputs(h):
        for a in range(2):
            output(h, a)

    summed = {}

    def add_pair(h, a):
        pair[h, a].wait_recv()
        half = slice(4 * h, 4 * h + 4)
        ps[a, half] = (pk[k, a, half].astype(F32) + sk[a, half].astype(F32)).astype(BF)

    def reduce_first():
        for a in range(2):
            add_pair(0, a)
        summed["far"] = remote(ps.at[:, pl.ds(2, 2)], pz, p4s.at[0], p4r.at[0], plane_peer(2, 0))

    def reduce_first_lo():
        summed["far"].wait_recv()
        pq[...] = (ps[:, 0:2].astype(F32) + pz[...].astype(F32)).astype(BF)
        summed["lo"] = remote(pq.at[:, 1 - yl], py, p4s.at[1], p4r.at[1], lo_peer)

    def reduce_second():
        for a in range(2):
            add_pair(1, a)
            for i, (t, dyl) in enumerate(((2, 0), (3, 0), (2, 1), (3, 1))):
                summed[a, i] = remote(ps.at[a, t * 2 + (yl + dyl) % 2], pr.at[i, a], p4s.at[2 + 4 * a + i],
                                      p4r.at[2 + 4 * a + i], plane_peer(OFFSETS[t], dyl))

    def grads(h, which):
        rows = slice(8 * h, 8 * h + 8)

        def put(acc, out, where, value):
            if h == 0:
                acc[where] = value
            else:
                out[where] = (acc[where] + value).astype(BF)

        for part, lo, width in ((all0, 0, CUT), (all1, CUT, G)):
            cols = slice(lo, lo + width)
            if which < 2:
                right = part[1 + which, rows].reshape(8 * B, width)
                for n in range(4):
                    feats = slice(n * 256, n * 256 + 256)
                    value = dot_rows(buf[0, rows, :, feats].reshape(8 * B, 256), right)
                    put((gate_acc, up_acc)[which], (gate_out, up_out)[which], (feats, cols), value)
            else:
                left = part[0, rows].reshape(8 * B, width)
                for n in range(4):
                    feats = slice(n * 256, n * 256 + 256)
                    value = dot_rows(left, buf[1, rows, :, feats].reshape(8 * B, 256))
                    put(down_acc, down_out, (cols, feats), value)

    def finish():
        summed["lo"].wait_recv()
        for a, out in enumerate((mixed_out, tg_out)):
            total = pq[a, yl].astype(F32) + py[a].astype(F32)
            for i in range(4):
                summed[a, i].wait_recv()
                total = total + pr[i, a].astype(F32)
            out[...] = total

    spread_first()
    for cp in weights:
        cp.wait()
    spread_last(0)
    ready(0, 0)
    x_tokens(0)
    spread_last(1)
    ready(0, 1)
    x_first(0)
    y_first(0)
    spread_second(0)
    spread_second(1)
    x_second(0)
    ready(1, 0)
    x_tokens(1)
    ready(1, 1)
    x_first(1)
    y_first(1)
    y_second(0)
    x_third(0)
    y_third(0)
    x_second(1)
    x_gather(0)
    y_gather(0)
    x_gather_second(0)
    y_second(1)
    x_third(1)
    y_forward(0)
    y_third(1)
    x_gather(1)
    x_forward(0)
    y_gather(1)
    y_forward_last(0)
    x_gather_second(1)
    y_forward(1)
    x_forward(1)
    x_done(0)
    y_done(0)
    outputs(0)
    y_forward_last(1)
    reduce_first()
    grads(0, 0)
    reduce_first_lo()
    x_done(1)
    y_done(1)
    outputs(1)
    reduce_second()
    grads(0, 1)
    grads(0, 2)
    for which in range(3):
        grads(1, which)
    finish()
    for cp in sends:
        cp.wait_send()


def body(tokens, gate_weight, up_weight, down_weight, cotangent):
    dma = lambda *shape: [pltpu.SemaphoreType.DMA(shape)] * 2
    vmem = lambda *shape: pltpu.VMEM(shape, BF)
    whole = pl.BlockSpec(memory_space=pltpu.HBM)
    mixed, token_grad, gate_total, up_total, down_total = pl.pallas_call(
        kernel,
        out_shape=(
            jax.ShapeDtypeStruct((B, D), F32),
            jax.ShapeDtypeStruct((B, D), F32),
            jax.ShapeDtypeStruct((D, F), BF),
            jax.ShapeDtypeStruct((D, F), BF),
            jax.ShapeDtypeStruct((F, D), BF),
        ),
        in_specs=[whole] * 5,
        out_specs=(pl.BlockSpec(memory_space=pltpu.VMEM),) * 5,
        scratch_shapes=[
            vmem(2, 16, B, D), vmem(D, F), vmem(D, F), vmem(F, D),
            vmem(2, 3, 8, B, CUT), vmem(2, 3, 8, B, G),
            vmem(2, 2, 3, B, CUT), vmem(2, 2, 3, B, CUT), vmem(2, 2, 3, B, CUT),
            vmem(2, 3, 2, B, CUT), vmem(2, 3, B, CUT),
            vmem(2, 4, 3, B, G), vmem(2, 4, 3, B, G),
            vmem(2, 3, 3, B, PIECE), vmem(2, 3, 3, B, G - PIECE),
            vmem(3, 16, B, CUT), vmem(3, 16, B, G),
            vmem(2, 2, 8, B, D), vmem(2, 8, B, D), vmem(2, 8, B, D),
            vmem(2, 2, B, D), vmem(2, 2, B, D), vmem(2, B, D), vmem(4, 2, B, D),
            pltpu.VMEM((D, F), F32), pltpu.VMEM((D, F), F32), pltpu.VMEM((F, D), F32),
            pltpu.SemaphoreType.DMA((3,)), pltpu.SemaphoreType.DMA((2,)),
            *dma(2, 7), *dma(2, 8),
            *dma(2, 2), *dma(2, 2), *dma(2, 2), *dma(2), *dma(2, 4), *dma(2, 3), *dma(2, 3),
            *dma(2), *dma(2, 2, 2), *dma(2, 2), *dma(2, 2), *dma(2, 2), *dma(2, 4),
            *dma(2, 2), *dma(10),
        ],
        compiler_params=pltpu.CompilerParams(
            collective_id=0, has_side_effects=True, vmem_limit_bytes=48 * 2**20
        ),
    )(tokens, cotangent, gate_weight, up_weight, down_weight)
    return (mixed, token_grad, gate_total.astype(F32), up_total.astype(F32), down_total.astype(F32))


def solution(mesh):
    placed = (
        P(("depth", "col"), "row"),
        P("row", ("col", "depth")),
        P("row", ("col", "depth")),
        P(("col", "depth"), "row"),
        P(("depth", "col"), "row"),
    )
    return jax.shard_map(
        body,
        mesh=mesh,
        in_specs=placed,
        out_specs=(
            P(("depth", "col"), "row"),
            P(("depth", "col"), "row"),
            P("row", ("col", "depth")),
            P("row", ("col", "depth")),
            P(("col", "depth"), "row"),
        ),
        check_vma=False,
    )
```

time: 852 us -> 116 us (0.14)
  waiting for transfers between devices: 751 us -> 0 us
  Pallas kernels: 0 us -> 106 us
  matrix products: 53.8 us -> 0 us
  blocking collectives: 14.9 us -> 0 us
  between operations: 14 us -> 0.65 us
    reduce_scatter x7 -> x0, waiting for transfers between devices: 404 us -> none  [the longest x1 96.8 us: body(): lax.psum_scatter(jnp.concatenate([product(segment, gate_panel), product(s...]
    all_gather x6 -> x0, waiting for transfers between devices: 343 us -> none  [the longest x1 72.3 us: body(): lax.all_gather(up_weight, 'depth', axis=1, tiled=True)]
    pallas_call x0 -> x1, Pallas kernels: none -> 106 us  [body(): pl.pallas_call(kernel, out_shape=(jax.ShapeDtypeStruct((B, D), F32), jax....]
    dot_general x9 -> x0, matrix products: 53.8 us -> none  [the longest x3 19.4 us: product_transposed(): lax.dot_general(left_side, right_side, (((1,), (1,)), ((), ())), preferre...]
    all_gather x2 -> x0, blocking collectives: 14.9 us -> none  [the longest x1 7.88 us: body(): lax.all_gather(cotangent, 'col', axis=0, tiled=True)]
  transfers between devices with their start and end apart: 13 -> 0, of which waited for: 13 -> 0; matrix products, arithmetic and copies ran while one was open for 8% -> 0% of each run, Pallas kernels for 0% -> 0%
where the time goes in v2:
time: 116 us
  Pallas kernels  106 us (91%)
  other arithmetic  6.4 us (6%)
  local copies, waits for them, and re-layouts  3.13 us (3%)
    pallas_call x1, Pallas kernels, body(): pl.pallas_call(kernel, out_shape=(jax.ShapeDtypeStruct((B, D), F32), jax....  106 us
    unnamed x6, local copies, waits for them, and re-layouts  3.13 us

profile of v2, /device:TPU:1, one launch (start us, length us, event | category | flops | bytes accessed | tf_op | source)
XLA Modules:
  0.0 116.3 jit_solution(1659622645510048194)
XLA Ops:
  0.6 0.0 copy-start
  0.6 0.9 copy-done
  1.5 0.0 copy-start.1
  1.5 0.9 copy-done.1
  2.4 106.1 %shard_map.92 = (f32[48,1024]{1,0:T(8,128)S(1)}, f32[48,1024]{1,0:T(8,128)S(1)}, bf16[1024,896]{1,0:T(8,128)(2,1)S(1)}, bf16[1024,896]{1,0:T(8,128)(2,1)S(1)}, bf16[896,1024]{1,0:T(8,128)(2,1)S(1)}) custom-call(bf16[48,1024]{1,0:T(8,128)(2,1)S(1)} %copy-done, bf16[48,1024]{1,0:T(8,128)(2,1)S(1)} %copy-done.1, bf16[1024,896]{1,0:T(8,128)(2,1)} %gw_in.1, ...), custom_call_target="tpu_custom_call" | custom-call | tf_op jit(solution)/shard_map/pallas_call | solution.py:401
  108.5 2.1 %convert_element_type.9 = f32[1024,896]{1,0:T(8,128)} convert(bf16[1024,896]{1,0:T(8,128)(2,1)S(1)} %get-tuple-element.12) | non-fusion elementwise | flops 917504 | bytes 5505024 | tf_op jit(solution)/shard_map/convert_element_type | solution.py:433
  110.6 2.1 %convert_element_type.10 = f32[1024,896]{1,0:T(8,128)} convert(bf16[1024,896]{1,0:T(8,128)(2,1)S(1)} %get-tuple-element.13) | non-fusion elementwise | flops 917504 | bytes 5505024 | tf_op jit(solution)/shard_map/convert_element_type | solution.py:433
  112.7 2.2 %convert_element_type.11 = f32[896,1024]{1,0:T(8,128)} convert(bf16[896,1024]{1,0:T(8,128)(2,1)S(1)} %get-tuple-element.14) | non-fusion elementwise | flops 917504 | bytes 5505024 | tf_op jit(solution)/shard_map/convert_element_type | solution.py:433
  114.9 0.7 copy.12
  115.6 0.7 copy.13
Async XLA Ops:
  0.6 0.9 copy-start
  1.5 0.9 copy-start.1

commit v3 on v2

--- a/solution.py
+++ b/solution.py
@@ -34,7 +34,7 @@
 def kernel(tok_in, cot_in, gw_in, uw_in, dw_in,
            mixed_out, tg_out, gate_out, up_out, down_out,
            buf, gw, uw, dw, part0, part1, xa, xd, xc, s0, r0y, y1, s1, ya, yb, all0, all1,
-           pk, sk, ps, pz, pq, py, pr, gate_acc, up_acc, down_acc,
+           pk, sk, ps, pz, pq, py, pr,
            w_sem, l_sem, p1s, p1r, fs, fr,
            xa_s, xa_r, xd_s, xd_r, xc_s, xc_r, r0y_s, r0y_r, y1_s, y1_r, ya_s, ya_r, yb_s, yb_r,
            g0y_s, g0y_r, g0x_s, g0x_r, g0f_s, g0f_r, g1x_s, g1x_r, g1f_s, g1f_r, g1y_s, g1y_r,
@@ -94,12 +94,12 @@
             own[a].wait()
             share("lo", a, 0, col, col, lo_peer)
             share("far", a, 1, col, 4 + col, plane_peer(2, 0))
+            share("far_lo", a, 6, col, 4 + col, plane_peer(2, 1))
             hand_on(a, 0, col)
         for a in range(2):
             moved["lo", a].wait_recv()
             hand_on(a, 1, mate)
             moved["far", a].wait_recv()
-            share("far_lo", a, 6, 4 + col, 4 + col, lo_peer)
             hand_on(a, 2, 4 + col)
             for i, (t, slot) in enumerate(((2, col), (3, col), (2, mate), (3, mate))):
                 share((t, i // 2), a, 2 + i, slot, 4 * t + slot, plane_peer(-OFFSETS[t], 0))
@@ -277,10 +277,6 @@
         half = pl.ds(4 * h, 4)
         pair[h, a] = remote(pk.at[1 - k, a, half], sk.at[a, half], ks.at[h, a], kr.at[h, a], sibling)
 
-    def outputs(h):
-        for a in range(2):
-            output(h, a)
-
     summed = {}
 
     def add_pair(h, a):
@@ -298,21 +294,18 @@
         pq[...] = (ps[:, 0:2].astype(F32) + pz[...].astype(F32)).astype(BF)
         summed["lo"] = remote(pq.at[:, 1 - yl], py, p4s.at[1], p4r.at[1], lo_peer)
 
-    def reduce_second():
-        for a in range(2):
-            add_pair(1, a)
-            for i, (t, dyl) in enumerate(((2, 0), (3, 0), (2, 1), (3, 1))):
-                summed[a, i] = remote(ps.at[a, t * 2 + (yl + dyl) % 2], pr.at[i, a], p4s.at[2 + 4 * a + i],
-                                      p4r.at[2 + 4 * a + i], plane_peer(OFFSETS[t], dyl))
+    def reduce_second(a):
+        add_pair(1, a)
+        for i, (t, dyl) in enumerate(((2, 0), (3, 0), (2, 1), (3, 1))):
+            summed[a, i] = remote(ps.at[a, t * 2 + (yl + dyl) % 2], pr.at[i, a], p4s.at[2 + 4 * a + i],
+                                  p4r.at[2 + 4 * a + i], plane_peer(OFFSETS[t], dyl))
 
     def grads(h, which):
         rows = slice(8 * h, 8 * h + 8)
-
-        def put(acc, out, where, value):
-            if h == 0:
-                acc[where] = value
-            else:
-                out[where] = (acc[where] + value).astype(BF)
+        out = (gate_out, up_out, down_out)[which]
+
+        def put(where, value):
+            out[where] = value if h == 0 else out[where] + value
 
         for part, lo, width in ((all0, 0, CUT), (all1, CUT, G)):
             cols = slice(lo, lo + width)
@@ -320,14 +313,12 @@
                 right = part[1 + which, rows].reshape(8 * B, width)
                 for n in range(4):
                     feats = slice(n * 256, n * 256 + 256)
-                    value = dot_rows(buf[0, rows, :, feats].reshape(8 * B, 256), right)
-                    put((gate_acc, up_acc)[which], (gate_out, up_out)[which], (feats, cols), value)
+                    put((feats, cols), dot_rows(buf[0, rows, :, feats].reshape(8 * B, 256), right))
             else:
                 left = part[0, rows].reshape(8 * B, width)
                 for n in range(4):
                     feats = slice(n * 256, n * 256 + 256)
-                    value = dot_rows(left, buf[1, rows, :, feats].reshape(8 * B, 256))
-                    put(down_acc, down_out, (cols, feats), value)
+                    put((cols, feats), dot_rows(left, buf[1, rows, :, feats].reshape(8 * B, 256)))
 
     def finish():
         summed["lo"].wait_recv()
@@ -342,70 +333,83 @@
     for cp in weights:
         cp.wait()
     spread_last(0)
+    spread_last(1)
     ready(0, 0)
     x_tokens(0)
-    spread_last(1)
     ready(0, 1)
     x_first(0)
     y_first(0)
     spread_second(0)
     spread_second(1)
-    x_second(0)
     ready(1, 0)
     x_tokens(1)
     ready(1, 1)
     x_first(1)
+    x_second(0)
     y_first(1)
     y_second(0)
+    y_third(0)
     x_third(0)
-    y_third(0)
     x_second(1)
+    y_gather(0)
+    y_second(1)
     x_gather(0)
-    y_gather(0)
+    y_third(1)
     x_gather_second(0)
-    y_second(1)
     x_third(1)
     y_forward(0)
-    y_third(1)
+    x_forward(0)
+    y_forward_last(0)
     x_gather(1)
-    x_forward(0)
+    x_done(0)
     y_gather(1)
-    y_forward_last(0)
+    y_done(0)
+    output(0, 0)
+    output(0, 1)
+    reduce_first()
     x_gather_second(1)
+    grads(0, 1)
     y_forward(1)
+    grads(0, 0)
+    grads(0, 2)
     x_forward(1)
-    x_done(0)
-    y_done(0)
-    outputs(0)
     y_forward_last(1)
-    reduce_first()
-    grads(0, 0)
     reduce_first_lo()
+    y_done(1)
     x_done(1)
-    y_done(1)
-    outputs(1)
-    reduce_second()
-    grads(0, 1)
-    grads(0, 2)
-    for which in range(3):
-        grads(1, which)
+    output(1, 0)
+    reduce_second(0)
+    output(1, 1)
+    reduce_second(1)
+    grads(1, 2)
+    grads(1, 0)
+    grads(1, 1)
     finish()
     for cp in sends:
         cp.wait_send()
+
+
+def write(*refs):
+    sems = refs[10]
+    copies = [pltpu.make_async_copy(refs[i], refs[5 + i], sems.at[i]) for i in (2, 3, 4, 0, 1)]
+    for cp in copies:
+        cp.start()
+    for cp in copies:
+        cp.wait()
 
 
 def body(tokens, gate_weight, up_weight, down_weight, cotangent):
     dma = lambda *shape: [pltpu.SemaphoreType.DMA(shape)] * 2
     vmem = lambda *shape: pltpu.VMEM(shape, BF)
     whole = pl.BlockSpec(memory_space=pltpu.HBM)
-    mixed, token_grad, gate_total, up_total, down_total = pl.pallas_call(
+    results = pl.pallas_call(
         kernel,
         out_shape=(
             jax.ShapeDtypeStruct((B, D), F32),
             jax.ShapeDtypeStruct((B, D), F32),
-            jax.ShapeDtypeStruct((D, F), BF),
-            jax.ShapeDtypeStruct((D, F), BF),
-            jax.ShapeDtypeStruct((F, D), BF),
+            jax.ShapeDtypeStruct((D, F), F32),
+            jax.ShapeDtypeStruct((D, F), F32),
+            jax.ShapeDtypeStruct((F, D), F32),
         ),
         in_specs=[whole] * 5,
         out_specs=(pl.BlockSpec(memory_space=pltpu.VMEM),) * 5,
@@ -419,7 +423,6 @@
             vmem(3, 16, B, CUT), vmem(3, 16, B, G),
             vmem(2, 2, 8, B, D), vmem(2, 8, B, D), vmem(2, 8, B, D),
             vmem(2, 2, B, D), vmem(2, 2, B, D), vmem(2, B, D), vmem(4, 2, B, D),
-            pltpu.VMEM((D, F), F32), pltpu.VMEM((D, F), F32), pltpu.VMEM((F, D), F32),
             pltpu.SemaphoreType.DMA((3,)), pltpu.SemaphoreType.DMA((2,)),
             *dma(2, 7), *dma(2, 8),
             *dma(2, 2), *dma(2, 2), *dma(2, 2), *dma(2), *dma(2, 4), *dma(2, 3), *dma(2, 3),
@@ -427,10 +430,18 @@
             *dma(2, 2), *dma(10),
         ],
         compiler_params=pltpu.CompilerParams(
-            collective_id=0, has_side_effects=True, vmem_limit_bytes=48 * 2**20
+            collective_id=0, has_side_effects=True, vmem_limit_bytes=38 * 2**20
         ),
-    )(tokens, cotangent, gate_weight, up_weight, down_weight)
-    return (mixed, token_grad, gate_total.astype(F32), up_total.astype(F32), down_total.astype(F32))
+    )(*(pltpu.with_memory_space_constraint(a, pltpu.HBM)
+        for a in (tokens, cotangent, gate_weight, up_weight, down_weight)))
+    return pl.pallas_call(
+        write,
+        out_shape=tuple(jax.ShapeDtypeStruct(r.shape, F32) for r in results),
+        in_specs=[pl.BlockSpec(memory_space=pltpu.VMEM)] * 5,
+        out_specs=(pl.BlockSpec(memory_space=pl.ANY),) * 5,
+        scratch_shapes=[pltpu.SemaphoreType.DMA((5,))],
+        compiler_params=pltpu.CompilerParams(vmem_limit_bytes=2**20),
+    )(*(pltpu.with_memory_space_constraint(r, pltpu.VMEM) for r in results))
 
 
 def solution(mesh):

time: 116 us -> 105 us (0.905)
  other arithmetic: 6.4 us -> 0 us
  local copies, waits for them, and re-layouts: 3.13 us -> 0 us
  Pallas kernels: 106 us -> 104 us
    convert_element_type x3 -> x0, other arithmetic: 6.4 us -> none  [the longest x1 2.25 us: body(): down_total.astype(F32)]
    pallas_call x1, Pallas kernels: 106 us -> 99.7 us  [body(): pl.pallas_call(kernel, out_shape=(jax.ShapeDtypeStruct((B, D), F32), jax....]
    pallas_call x0 -> x1, Pallas kernels: none -> 4.3 us  [body(): pl.pallas_call(write, out_shape=tuple((jax.ShapeDtypeStruct(r.shape, F32)...]
    unnamed x6 -> x0, local copies, waits for them, and re-layouts: 3.13 us -> none
where the time goes in v3:
time: 105 us
  Pallas kernels  104 us (99%)
    pallas_call x1, Pallas kernels, body(): pl.pallas_call(kernel, out_shape=(jax.ShapeDtypeStruct((B, D), F32), jax....  99.7 us
    pallas_call x1, Pallas kernels, body(): pl.pallas_call(write, out_shape=tuple((jax.ShapeDtypeStruct(r.shape, F32)...  4.3 us

profile of v3, /device:TPU:1, one launch (start us, length us, event | category | flops | bytes accessed | tf_op | source)
XLA Modules:
  0.0 104.8 jit_solution(14062981191720107210)
XLA Ops:
  0.6 99.7 %shard_map.92 = (f32[48,1024]{1,0:T(8,128)S(1)}, f32[48,1024]{1,0:T(8,128)S(1)}, f32[1024,896]{1,0:T(8,128)S(1)}, f32[1024,896]{1,0:T(8,128)S(1)}, f32[896,1024]{1,0:T(8,128)S(1)}) custom-call(bf16[48,1024]{1,0:T(8,128)(2,1)} %tok_in.1, bf16[48,1024]{1,0:T(8,128)(2,1)} %cot_in.1, bf16[1024,896]{1,0:T(8,128)(2,1)} %gw_in.1, bf16[1024,896]{1,0:T(8,128)(2,1)} %uw_in.1, ...), custom_call_target="tpu_custom_call" | custom-call | tf_op jit(solution)/shard_map/pallas_call | solution.py:405
  100.4 4.3 %shard_map.93 = (f32[48,1024]{1,0:T(8,128)}, f32[48,1024]{1,0:T(8,128)}, f32[1024,896]{1,0:T(8,128)}, f32[1024,896]{1,0:T(8,128)}, f32[896,1024]{1,0:T(8,128)}) custom-call(f32[48,1024]{1,0:T(8,128)S(1)} %get-tuple-element.10.refs_0_, f32[48,1024]{1,0:T(8,128)S(1)} %get-tuple-element.11.refs_1_, f32[1024,896]{1,0:T(8,128)S(1)} %get-tuple-element.12.refs_2_, ...), custom_call_target="tpu_custom_call" | custom-call | tf_op jit(solution)/shard_map/pallas_call | solution.py:437

commit v4 on v3

--- a/solution.py
+++ b/solution.py
@@ -94,12 +94,12 @@
             own[a].wait()
             share("lo", a, 0, col, col, lo_peer)
             share("far", a, 1, col, 4 + col, plane_peer(2, 0))
-            share("far_lo", a, 6, col, 4 + col, plane_peer(2, 1))
             hand_on(a, 0, col)
         for a in range(2):
             moved["lo", a].wait_recv()
             hand_on(a, 1, mate)
             moved["far", a].wait_recv()
+            share("far_lo", a, 6, 4 + col, 4 + col, lo_peer)
             hand_on(a, 2, 4 + col)
             for i, (t, slot) in enumerate(((2, col), (3, col), (2, mate), (3, mate))):
                 share((t, i // 2), a, 2 + i, slot, 4 * t + slot, plane_peer(-OFFSETS[t], 0))
@@ -140,22 +140,22 @@
     def x_tokens(h):
         tokens_part(h, part0, 0, CUT)
 
-    def x_first(h):
+    def x_alpha(h):
         cotangent_part(h, part0, 0, CUT)
         cxa[h] = [remote(part0.at[h, :, x_at(2) * 2 + i], xa.at[h, i], xa_s.at[h, i], xa_r.at[h, i], x_peer(1 - 2 * i))
                   for i in range(2)]
+
+    def x_direct(h):
         cxd[h] = [remote(part0.at[h, :, x_at(1 - 2 * i) * 2 + 1 - i], xd.at[h, i], xd_s.at[h, i], xd_r.at[h, i],
                          x_peer(1 - 2 * i)) for i in range(2)]
 
-    def x_second(h):
-        cxc[h] = []
-        for i in range(2):
-            cxa[h][i].wait_recv()
-            xa[h, i] = (xa[h, i].astype(F32) + part0[h, :, x_at(1 - 2 * i) * 2 + i].astype(F32)).astype(BF)
-            cxc[h].append(remote(xa.at[h, i], xc.at[h, i], xc_s.at[h, i], xc_r.at[h, i], x_peer(1 - 2 * i)))
+    def x_second(h, i):
+        cxa[h][i].wait_recv()
+        xa[h, i] = (xa[h, i].astype(F32) + part0[h, :, x_at(1 - 2 * i) * 2 + i].astype(F32)).astype(BF)
+        cxc[h, i] = remote(xa.at[h, i], xc.at[h, i], xc_s.at[h, i], xc_r.at[h, i], x_peer(1 - 2 * i))
 
     def x_third(h):
-        for cp in cxd[h] + cxc[h]:
+        for cp in cxd[h] + [cxc[h, 0], cxc[h, 1]]:
             cp.wait_recv()
         for i in range(2):
             s0[h, :, i] = (part0[h, :, x * 2 + i].astype(F32) + xd[h, 1 - i].astype(F32)
@@ -164,12 +164,14 @@
 
     cy1, cya, cyb = {}, {}, {}
 
-    def y_first(h):
+    def y_partial(h):
         tokens_part(h, part1, CUT, G)
         cotangent_part(h, part1, CUT, G)
-        cy1[h] = {j: remote(part1.at[h, :, (1 - yh) * 4 + x_at(turn * j)], y1.at[h, j], y1_s.at[h, j], y1_r.at[h, j],
-                            y_peer) for j in (2, 1, 3, 0)}
         cya[h], cyb[h] = {}, {}
+
+    def y_send(h, j):
+        cy1[h, j] = remote(part1.at[h, :, (1 - yh) * 4 + x_at(turn * j)], y1.at[h, j], y1_s.at[h, j], y1_r.at[h, j],
+                           y_peer)
 
     def lap(h, kind, src, ways):
         if "a" in ways:
@@ -179,24 +181,21 @@
             cyb[h][kind] = remote(src.at[:, :, pl.ds(PIECE, G - PIECE)], yb.at[h, kind], yb_s.at[h, kind],
                                   yb_r.at[h, kind], x_peer(-turn if kind != 1 else turn))
 
-    def y_second(h):
-        for j in (2, 1, 3, 0):
-            cy1[h][j].wait_recv()
-            s1[h, j] = (part1[h, :, yh * 4 + x_at(turn * j)].astype(F32) + y1[h, j].astype(F32)).astype(BF)
-            if j == 2:
-                lap(h, 0, s1.at[h, 2], "ab")
-            elif j == 1:
-                lap(h, 1, s1.at[h, 1], "b")
-            elif j == 3:
-                lap(h, 1, s1.at[h, 3], "a")
-
-    def y_third(h):
-        cya[h][0].wait_recv()
-        s1[h, 1, :, :, :PIECE] = (s1[h, 1, :, :, :PIECE].astype(F32) + ya[h, 0].astype(F32)).astype(BF)
-        lap(h, 2, s1.at[h, 1], "a")
-        cyb[h][0].wait_recv()
-        s1[h, 3, :, :, PIECE:] = (s1[h, 3, :, :, PIECE:].astype(F32) + yb[h, 0].astype(F32)).astype(BF)
-        lap(h, 2, s1.at[h, 3], "b")
+    def y_sum(h, j):
+        cy1[h, j].wait_recv()
+        s1[h, j] = (part1[h, :, yh * 4 + x_at(turn * j)].astype(F32) + y1[h, j].astype(F32)).astype(BF)
+        if j:
+            lap(h, j % 2, s1.at[h, j], ("b", "ab", "a")[j - 1])
+
+    def y_third(h, i):
+        if i == 0:
+            cya[h][0].wait_recv()
+            s1[h, 1, :, :, :PIECE] = (s1[h, 1, :, :, :PIECE].astype(F32) + ya[h, 0].astype(F32)).astype(BF)
+            lap(h, 2, s1.at[h, 1], "a")
+        else:
+            cyb[h][0].wait_recv()
+            s1[h, 3, :, :, PIECE:] = (s1[h, 3, :, :, PIECE:].astype(F32) + yb[h, 0].astype(F32)).astype(BF)
+            lap(h, 2, s1.at[h, 3], "b")
 
     cg0y, cg0x, cg0f, cg1x, cg1f, cg1y = {}, {}, {}, {}, {}, {}
 
@@ -216,10 +215,10 @@
         cg0y[h].wait_recv()
         gather0(h, h * 8 + x * 2 + 1 - yh, 1)
 
-    def x_forward(h):
-        for i, slot in enumerate((h * 8 + x_at(-1) * 2 + yh, h * 8 + x_at(1) * 2 + 1 - yh)):
-            cg0x[h, i, i].wait_recv()
-            cg0f[h, i] = remote(all0.at[:, slot], all0.at[:, slot], g0f_s.at[h, i], g0f_r.at[h, i], x_peer(1 - 2 * i))
+    def x_forward(h, i):
+        slot = h * 8 + (x_at(-1) * 2 + yh if i == 0 else x_at(1) * 2 + 1 - yh)
+        cg0x[h, i, i].wait_recv()
+        cg0f[h, i] = remote(all0.at[:, slot], all0.at[:, slot], g0f_s.at[h, i], g0f_r.at[h, i], x_peer(1 - 2 * i))
 
     def x_done(h):
         for cp in (cg0x[h, 0, 1], cg0x[h, 1, 0], cg0f[h, 0], cg0f[h, 1]):
@@ -241,13 +240,13 @@
                                 x_peer(turn * (1 - 2 * i)))
         to_y(h, 0, slot)
 
-    def y_forward(h):
-        for i, (lo, width) in enumerate(((0, PIECE), (PIECE, G - PIECE))):
-            slot = h * 8 + yh * 4 + x_at(turn * (2 * i - 1))
-            cg1x[h, i].wait_recv()
-            piece = all1.at[:, slot, :, pl.ds(lo, width)]
-            cg1f[h, i] = remote(piece, piece, g1f_s.at[h, i], g1f_r.at[h, i], x_peer(turn * (1 - 2 * i)))
-            to_y(h, 3 - 2 * i, slot)
+    def y_forward(h, i):
+        lo, width = ((0, PIECE), (PIECE, G - PIECE))[i]
+        slot = h * 8 + yh * 4 + x_at(turn * (2 * i - 1))
+        cg1x[h, i].wait_recv()
+        piece = all1.at[:, slot, :, pl.ds(lo, width)]
+        cg1f[h, i] = remote(piece, piece, g1f_s.at[h, i], g1f_r.at[h, i], x_peer(turn * (1 - 2 * i)))
+        to_y(h, 3 - 2 * i, slot)
 
     def y_forward_last(h):
         for i in range(2):
@@ -337,52 +336,76 @@
     ready(0, 0)
     x_tokens(0)
     ready(0, 1)
-    x_first(0)
-    y_first(0)
+    y_partial(0)
+    y_send(0, 0)
+    x_alpha(0)
     spread_second(0)
+    ready(1, 0)
     spread_second(1)
-    ready(1, 0)
+    y_send(0, 3)
+    y_send(0, 1)
+    ready(1, 1)
+    y_send(0, 2)
+    x_direct(0)
+    x_second(0, 0)
+    x_second(0, 1)
     x_tokens(1)
-    ready(1, 1)
-    x_first(1)
-    x_second(0)
-    y_first(1)
-    y_second(0)
-    y_third(0)
+    y_partial(1)
+    y_send(1, 1)
+    x_alpha(1)
+    y_sum(0, 1)
+    y_sum(0, 2)
+    x_direct(1)
+    y_send(1, 0)
     x_third(0)
-    x_second(1)
+    y_sum(0, 3)
+    y_third(0, 1)
+    x_second(1, 0)
+    y_sum(1, 1)
+    x_second(1, 1)
+    y_send(1, 2)
+    y_third(0, 0)
+    y_sum(0, 0)
+    y_send(1, 3)
+    x_gather(0)
     y_gather(0)
-    y_second(1)
-    x_gather(0)
-    y_third(1)
     x_gather_second(0)
+    y_sum(1, 2)
     x_third(1)
-    y_forward(0)
-    x_forward(0)
+    y_forward(0, 0)
+    y_sum(1, 0)
+    y_forward(0, 1)
+    y_sum(1, 3)
+    y_third(1, 0)
+    y_third(1, 1)
+    x_forward(0, 1)
+    x_forward(0, 0)
     y_forward_last(0)
+    y_gather(1)
     x_gather(1)
     x_done(0)
-    y_gather(1)
     y_done(0)
     output(0, 0)
     output(0, 1)
     reduce_first()
+    y_forward(1, 0)
+    y_forward(1, 1)
     x_gather_second(1)
     grads(0, 1)
-    y_forward(1)
-    grads(0, 0)
-    grads(0, 2)
-    x_forward(1)
     y_forward_last(1)
+    x_forward(1, 0)
+    x_forward(1, 1)
     reduce_first_lo()
     y_done(1)
     x_done(1)
     output(1, 0)
     reduce_second(0)
     output(1, 1)
+    grads(0, 2)
     reduce_second(1)
+    grads(0, 0)
+    grads(1, 0)
     grads(1, 2)
-    grads(1, 0)
     grads(1, 1)
     finish()
     for cp in sends:

time: 105 us -> 102 us (0.971)
  Pallas kernels: 104 us -> 101 us
    pallas_call x1, Pallas kernels: 99.7 us -> 96.9 us  [body(): pl.pallas_call(kernel, out_shape=(jax.ShapeDtypeStruct((B, D), F32), jax....]
where the time goes in v4:
time: 102 us
  Pallas kernels  101 us (99%)
    pallas_call x1, Pallas kernels, body(): pl.pallas_call(kernel, out_shape=(jax.ShapeDtypeStruct((B, D), F32), jax....  96.9 us
    pallas_call x1, Pallas kernels, body(): pl.pallas_call(write, out_shape=tuple((jax.ShapeDtypeStruct(r.shape, F32)...  4.3 us

profile of v4, /device:TPU:1, one launch (start us, length us, event | category | flops | bytes accessed | tf_op | source)
XLA Modules:
  0.0 102.0 jit_solution(3036424088795538845)
XLA Ops:
  0.6 96.9 %shard_map.92 = (f32[48,1024]{1,0:T(8,128)S(1)}, f32[48,1024]{1,0:T(8,128)S(1)}, f32[1024,896]{1,0:T(8,128)S(1)}, f32[1024,896]{1,0:T(8,128)S(1)}, f32[896,1024]{1,0:T(8,128)S(1)}) custom-call(bf16[48,1024]{1,0:T(8,128)(2,1)} %tok_in.1, bf16[48,1024]{1,0:T(8,128)(2,1)} %cot_in.1, bf16[1024,896]{1,0:T(8,128)(2,1)} %gw_in.1, bf16[1024,896]{1,0:T(8,128)(2,1)} %uw_in.1, ...), custom_call_target="tpu_custom_call" | custom-call | tf_op jit(solution)/shard_map/pallas_call | solution.py:428
  97.5 4.3 %shard_map.93 = (f32[48,1024]{1,0:T(8,128)}, f32[48,1024]{1,0:T(8,128)}, f32[1024,896]{1,0:T(8,128)}, f32[1024,896]{1,0:T(8,128)}, f32[896,1024]{1,0:T(8,128)}) custom-call(f32[48,1024]{1,0:T(8,128)S(1)} %get-tuple-element.10.refs_0_, f32[48,1024]{1,0:T(8,128)S(1)} %get-tuple-element.11.refs_1_, f32[1024,896]{1,0:T(8,128)S(1)} %get-tuple-element.12.refs_2_, ...), custom_call_target="tpu_custom_call" | custom-call | tf_op jit(solution)/shard_map/pallas_call | solution.py:460

commit v5 on v4

--- a/solution.py
+++ b/solution.py
@@ -16,6 +16,7 @@
 F = 896
 CUT = 512
 G = F - CUT
+PARTS = 4
 PIECE = 256
 
 
@@ -414,7 +415,14 @@
 
 def write(*refs):
     sems = refs[10]
-    copies = [pltpu.make_async_copy(refs[i], refs[5 + i], sems.at[i]) for i in (2, 3, 4, 0, 1)]
+    copies = []
+    for i in range(2, 5):
+        rows = refs[i].shape[0] // PARTS
+        for n in range(PARTS):
+            part = pl.ds(n * rows, rows)
+            copies.append((refs[i].at[part], refs[5 + i].at[part]))
+    copies += [(refs[i], refs[5 + i]) for i in range(2)]
+    copies = [pltpu.make_async_copy(a, b, sems.at[n]) for n, (a, b) in enumerate(copies)]
     for cp in copies:
         cp.start()
     for cp in copies:
@@ -462,7 +470,7 @@
         out_shape=tuple(jax.ShapeDtypeStruct(r.shape, F32) for r in results),
         in_specs=[pl.BlockSpec(memory_space=pltpu.VMEM)] * 5,
         out_specs=(pl.BlockSpec(memory_space=pl.ANY),) * 5,
-        scratch_shapes=[pltpu.SemaphoreType.DMA((5,))],
+        scratch_shapes=[pltpu.SemaphoreType.DMA((3 * PARTS + 2,))],
         compiler_params=pltpu.CompilerParams(vmem_limit_bytes=2**20),
     )(*(pltpu.with_memory_space_constraint(r, pltpu.VMEM) for r in results))
 

time: 102 us -> 102 us (level)
  no operation moved by 1% of the time
where the time goes in v5:
time: 102 us
  Pallas kernels  101 us (99%)
    pallas_call x1, Pallas kernels, body(): pl.pallas_call(kernel, out_shape=(jax.ShapeDtypeStruct((B, D), F32), jax....  96.9 us
    pallas_call x1, Pallas kernels, body(): pl.pallas_call(write, out_shape=tuple((jax.ShapeDtypeStruct(r.shape, F32)...  4.3 us

profile of v5, /device:TPU:1, one launch (start us, length us, event | category | flops | bytes accessed | tf_op | source)
XLA Modules:
  0.0 102.0 jit_solution(4860019540837559605)
XLA Ops:
  0.6 96.9 %shard_map.92 = (f32[48,1024]{1,0:T(8,128)S(1)}, f32[48,1024]{1,0:T(8,128)S(1)}, f32[1024,896]{1,0:T(8,128)S(1)}, f32[1024,896]{1,0:T(8,128)S(1)}, f32[896,1024]{1,0:T(8,128)S(1)}) custom-call(bf16[48,1024]{1,0:T(8,128)(2,1)} %tok_in.1, bf16[48,1024]{1,0:T(8,128)(2,1)} %cot_in.1, bf16[1024,896]{1,0:T(8,128)(2,1)} %gw_in.1, bf16[1024,896]{1,0:T(8,128)(2,1)} %uw_in.1, ...), custom_call_target="tpu_custom_call" | custom-call | tf_op jit(solution)/shard_map/pallas_call | solution.py:436
  97.5 4.3 %shard_map.93 = (f32[48,1024]{1,0:T(8,128)}, f32[48,1024]{1,0:T(8,128)}, f32[1024,896]{1,0:T(8,128)}, f32[1024,896]{1,0:T(8,128)}, f32[896,1024]{1,0:T(8,128)}) custom-call(f32[48,1024]{1,0:T(8,128)S(1)} %get-tuple-element.10.refs_0_, f32[48,1024]{1,0:T(8,128)S(1)} %get-tuple-element.11.refs_1_, f32[1024,896]{1,0:T(8,128)S(1)} %get-tuple-element.12.refs_2_, ...), custom_call_target="tpu_custom_call" | custom-call | tf_op jit(solution)/shard_map/pallas_call | solution.py:468
